TPU v7x, 32 devices: a whole 2x2x4 slice. The times are simulated.
32 devices in a mesh: rows: 8 (over y, x, core), cols: 4 (over z).
Axes of the slice: x: 2, y: 2, z: 4, core: 2. Of those that a mesh axis runs over, the one named last changes fastest.
Arguments:
- greens: bfloat16 [512, 65536], P('cols', 'rows'), may hold values from -0.5 to 0.5
- slip_values: bfloat16 [2048, 128], P('cols'), may hold values from 0.5 to 4
- rupture_ids: int32 [2048, 128], P('cols'), may hold values from -1 to 511, as said below
- win_point: int32 [1024], P('rows'), may hold values from 0 to 255, never falling along the last dimension, each value on 1 to 32 neighbouring positions
Outputs:
- window_peak: float32 [2048, 1024], P('cols', 'rows')
Inputs may be any that keep to these rules, and one draw needn't show every extreme that they name: `rupture_ids`: each row lists its sources as one run of consecutive source numbers in its first slots and -1 in the rest; some row fills all 128 slots. `win_point`: never falls along the windows; every point holds 1 to 32 consecutive windows and some point exactly 32.
All inputs are finite; a program needn't handle non-finite values.
Results may differ from a plain program's by a relative error of at most 0.0003.
Values may be sent and summed in bfloat16 or wider, within the bound.
A program may use at most 64 MiB of HBM per device.

v0:
```python
import functools
import math

import jax
import jax.numpy as jnp
from jax import lax
from jax.experimental import pallas as pl
from jax.experimental.pallas import tpu as pltpu
from jax.sharding import PartitionSpec as P

TSTEP = 64
MOST = 32
LANES = 128
META = 16
CHUNKS = 8
MESH = pl.DeviceIdType.MESH


def extended(cells, sides, width):
    for axis, dim in sides:
        count = lax.axis_size(axis)
        ends = count - 1
        head = lax.slice_in_dim(cells, 0, width, axis=dim)
        tail = lax.slice_in_dim(cells, cells.shape[dim] - width, cells.shape[dim], axis=dim)
        cells = jnp.concatenate(
            [
                lax.ppermute(tail, axis, [(i, (i + 1) % count) for i in range(ends)]),
                cells,
                lax.ppermute(head, axis, [((i + 1) % count, i) for i in range(ends)]),
            ],
            axis=dim,
        )
    return cells


def spread_slips(slip_values, source_ids, width):
    count = source_ids.shape[0]
    slots = source_ids.shape[1]
    group = math.gcd(count, 64)
    sources = jnp.arange(width, dtype=jnp.int32)[None, None, :]
    values_grouped = slip_values.reshape(count // group, group, slots)
    ids_grouped = source_ids.reshape(count // group, group, slots)

    def one_group(operands):
        values, ids = operands
        onehot = (ids[:, :, None] == sources).astype(jnp.bfloat16)
        return jnp.einsum("kl,kls->ks", values, onehot, preferred_element_type=jnp.float32).astype(
            jnp.bfloat16
        )

    return lax.map(one_group, (values_grouped, ids_grouped)).reshape(count, width)


def window_maxima(dense, panel):
    scenarios = dense.shape[0]
    windows = panel.shape[1] // TSTEP
    group = math.gcd(windows, max(1, 512 // TSTEP))
    turns = windows // group
    span = group * TSTEP

    def one_turn(turn):
        piece = lax.dynamic_slice_in_dim(panel, turn * span, span, 1)
        wave = jnp.dot(dense, piece, preferred_element_type=jnp.float32)
        return jnp.max(wave.reshape(scenarios, group, TSTEP), axis=2)

    stacked = lax.map(one_turn, jnp.arange(turns, dtype=jnp.int32))
    return jnp.transpose(stacked, (1, 0, 2)).reshape(scenarios, windows)


def combine(earlier, later):
    flag = jnp.logical_or(earlier[0], later[0])
    value = jnp.where(later[0], later[1], jnp.maximum(earlier[1], later[1]))
    return (flag, value)


def general(greens, slip_values, rupture_ids, win_point):
    width = greens.shape[0] * lax.axis_size("cols")
    share = lax.all_to_all(greens, "cols", split_axis=1, concat_axis=0, tiled=True)
    dense = spread_slips(slip_values, rupture_ids, width)
    every = lax.all_gather(dense, "cols", axis=0, tiled=True)
    total = every.shape[0]
    scen_group = math.gcd(total, 512)
    grouped = every.reshape(total // scen_group, scen_group, width)

    def per_group(slip_group):
        return window_maxima(slip_group, share)

    partial_max = lax.map(per_group, grouped).reshape(total, share.shape[1] // TSTEP)
    window_max = lax.all_to_all(partial_max, "cols", split_axis=0, concat_axis=1, tiled=True)
    windows = window_max.shape[1]
    begins = jnp.concatenate([jnp.ones((1,), bool), win_point[1:] != win_point[:-1]])
    finals = jnp.concatenate([win_point[:-1] != win_point[1:], jnp.ones((1,), bool)])
    begin_flags = jnp.broadcast_to(begins[None, :], window_max.shape)
    final_flags = jnp.broadcast_to(finals[None, :], window_max.shape)
    forward = lax.associative_scan(combine, (begin_flags, window_max), axis=1)[1]
    backward = lax.associative_scan(combine, (final_flags, window_max), reverse=True, axis=1)[1]
    local_peak = jnp.maximum(forward, backward)
    edge_values = jnp.stack([backward[:, 0], forward[:, windows - 1]], axis=1)
    edge_points = jnp.stack([win_point[0] + 1, win_point[windows - 1] + 1]).astype(jnp.float32)[
        None, :
    ]
    padded_values, padded_points = (
        extended(edge_values, (("rows", 1),), 1),
        extended(edge_points, (("rows", 1),), 1),
    )
    point_code = (win_point + 1).astype(jnp.float32)[None, :]
    from_left = jnp.maximum(local_peak, padded_values[:, 0:1])
    local_peak = jnp.where(point_code == padded_points[0, 0], from_left, local_peak)
    from_right = jnp.maximum(local_peak, padded_values[:, 3:4])
    local_peak = jnp.where(point_code == padded_points[0, 3], from_right, local_peak)
    return local_peak


def kernel(
    n, count, g_hbm, v_hbm, id_hbm, wp_hbm, out_ref,
    g_ref, v_ref, id_ref, wp_ref, panel, sent, slip, weights, res, home, edge, points,
    gload, load, gsend, grecv, zsend, zrecv, psend, precv, rsend, rrecv, wsend, wrecv, esend, erecv,
):
    f32, bf16 = jnp.float32, jnp.bfloat16
    me = lax.axis_index("rows")
    z = lax.axis_index("cols")
    width, rows = g_ref.shape
    half = rows // 2
    span = half // CHUNKS
    wspan = span // TSTEP
    whalf = half // TSTEP
    kloc = home.shape[2]
    planes = count // 2
    share = kloc // planes
    chip, core = me // 2, lax.rem(me, 2)
    left, right = lax.rem(me + count - 1, count), lax.rem(me + 1, count)
    odd = lax.rem(z, 2)

    barrier = pltpu.get_barrier_semaphore()
    for d in range(1, n):
        pl.semaphore_signal(barrier, inc=1, device_id={"cols": lax.rem(z + d, n)}, device_id_type=MESH)
    for d in range(1, planes):
        pl.semaphore_signal(
            barrier, inc=1, device_id={"rows": lax.rem(chip + d, planes) * 2 + core}, device_id_type=MESH
        )
    for other in (left, right):
        pl.semaphore_signal(barrier, inc=1, device_id={"rows": other}, device_id_type=MESH)

    def chunk(parity, t):
        return t + parity * (CHUNKS - 1 - 2 * t)

    def columns(parity, t):
        return pl.ds(pl.multiple_of(parity * half + chunk(parity, t) * span, span), span)

    def green_load(which, t):
        parity = 1 - odd if which == 0 else odd
        place = columns(parity, t)
        return pltpu.make_async_copy(g_hbm.at[:, place], g_ref.at[:, place], gload.at[which, t])

    mine = pl.ds(pl.multiple_of(chip * share, share), share)
    loads = [
        pltpu.make_async_copy(id_hbm.at[mine, :], id_ref, load.at[0]),
        pltpu.make_async_copy(v_hbm.at[mine, :], v_ref, load.at[1]),
        pltpu.make_async_copy(wp_hbm, wp_ref, load.at[2]),
    ]
    for copy in loads:
        copy.start()
    for which in range(2):
        for t in range(CHUNKS):
            green_load(which, t).start()
    for copy in loads:
        copy.wait()
    ids = id_ref[...]
    values = jnp.where(ids >= 0, v_ref[...].astype(f32), 0.0)
    start = jnp.broadcast_to(jnp.maximum(ids[:, 0:1], 0), ids.shape)
    shift = lax.rem(start, width)
    block = start // width
    step = 1
    while step < width:
        moved = pltpu.roll(values, step, 1)
        values = jnp.where(lax.rem(shift // step, 2) == 1, moved, values)
        step *= 2
    slip[z, 0:width, mine] = values.T.astype(bf16)
    shift_rows = shift.astype(f32).T[0:META, :]
    block_rows = block.astype(f32).T[0:META, :]
    first = lax.broadcasted_iota(jnp.int32, (META, share), 0) < META // 2
    slip[z, width : width + META, mine] = jnp.where(first, shift_rows, block_rows).astype(bf16)
    points[0] = jnp.broadcast_to(wp_ref[...].astype(f32), (8, wp_ref.shape[1]))

    pl.semaphore_wait(barrier, n - 1 + planes - 1 + 2)

    def slip_copy(target, source):
        return pltpu.make_async_remote_copy(
            src_ref=slip.at[z, :, mine], dst_ref=slip.at[z, :, mine],
            send_sem=zsend.at[target], recv_sem=zrecv.at[source],
            device_id={"cols": target}, device_id_type=MESH,
        )

    def plane_copy(target, source):
        place = slip.at[:, :, pl.ds(pl.multiple_of(source * share, share), share)]
        return pltpu.make_async_remote_copy(
            src_ref=place, dst_ref=place, send_sem=psend.at[target], recv_sem=precv.at[source],
            device_id={"rows": target * 2 + core}, device_id_type=MESH,
        )

    def green_copy(side, t, parity):
        place = pl.ds(pl.multiple_of(chunk(parity, t) * span, span), span)
        to, at = (lax.rem(z + n - 1, n), 2 * width) if side == 0 else (lax.rem(z + 1, n), 0)
        return pltpu.make_async_remote_copy(
            src_ref=sent.at[place, :], dst_ref=panel.at[place, pl.ds(at, width)],
            send_sem=gsend.at[side, t], recv_sem=grecv.at[side, t],
            device_id={"cols": to}, device_id_type=MESH,
        )

    def result_copy(t, target, source, parity):
        place = pl.ds(pl.multiple_of(chunk(parity, t) * wspan, wspan), wspan)
        return pltpu.make_async_remote_copy(
            src_ref=res.at[place, pl.ds(pl.multiple_of(target * kloc, kloc), kloc)],
            dst_ref=home.at[source, place, :],
            send_sem=rsend.at[t, target], recv_sem=rrecv.at[t, source],
            device_id={"cols": target}, device_id_type=MESH,
        )

    def row_copies(src_left, src_right, buffer, send, recv):
        to_left = pltpu.make_async_remote_copy(
            src_ref=src_left, dst_ref=buffer.at[2], send_sem=send.at[0], recv_sem=recv.at[0],
            device_id={"rows": left}, device_id_type=MESH,
        )
        to_right = pltpu.make_async_remote_copy(
            src_ref=src_right, dst_ref=buffer.at[1], send_sem=send.at[1], recv_sem=recv.at[1],
            device_id={"rows": right}, device_id_type=MESH,
        )
        return to_left, to_right

    for d in range(1, n):
        slip_copy(lax.rem(z + d, n), z).start()

    def send(t, carry):
        green_load(0, t).wait()
        place = pl.ds(pl.multiple_of(chunk(1 - odd, t) * span, span), span)
        sent[place, :] = g_ref[:, columns(1 - odd, t)].T

        @pl.when(z > 0)
        def _():
            green_copy(0, t, 1 - odd).start()

        @pl.when(z < n - 1)
        def _():
            green_copy(1, t, 1 - odd).start()

        return carry

    lax.fori_loop(0, CHUNKS, send, 0)

    point_copies = row_copies(points.at[0], points.at[0], points, wsend, wrecv)
    for copy in point_copies:
        copy.start()
    for d in range(1, n):
        slip_copy(lax.rem(z + d, n), lax.rem(z + d, n)).wait_recv()
    for d in range(1, planes):
        plane_copy(lax.rem(chip + d, planes), chip).start()

    def keep(t, carry):
        green_load(1, t).wait()
        place = pl.ds(pl.multiple_of(chunk(odd, t) * span, span), span)
        panel[place, width : 2 * width] = g_ref[:, columns(odd, t)].T
        return carry

    lax.fori_loop(0, CHUNKS, keep, 0)

    @pl.when(z == 0)
    def _():
        panel[:, 0:width] = jnp.zeros((half, width), bf16)

    @pl.when(z == n - 1)
    def _():
        panel[:, 2 * width : 3 * width] = jnp.zeros((half, width), bf16)

    for d in range(1, planes):
        source = lax.rem(chip + d, planes)
        plane_copy(source, source).wait_recv()

    for q in range(n):
        at = slice(q * kloc, (q + 1) * kloc)
        folded = slip[q, 0:width, :].astype(f32)
        meta = slip[q, width : width + META, :].astype(f32)
        shifts, blocks = meta[0:1, :], meta[META // 2 : META // 2 + 1, :]
        later = lax.broadcasted_iota(jnp.int32, folded.shape, 0).astype(f32) >= shifts
        upper = jnp.where(later, folded, 0.0)
        lower = jnp.where(later, 0.0, folded)
        for i in range(3):
            which = (z + i - 1).astype(f32)
            dense = jnp.where(blocks == which, upper, 0.0) + jnp.where(blocks + 1.0 == which, lower, 0.0)
            weights[i * width : (i + 1) * width, at] = dense.astype(bf16)

    own = pl.ds(pl.multiple_of(z * kloc, kloc), kloc)

    def compute(t, carry):
        @pl.when(z > 0)
        def _():
            green_copy(1, t, odd).wait_recv()

        @pl.when(z < n - 1)
        def _():
            green_copy(0, t, odd).wait_recv()

        place = pl.ds(pl.multiple_of(chunk(odd, t) * span, span), span)
        wplace = pl.ds(pl.multiple_of(chunk(odd, t) * wspan, wspan), wspan)
        for q in range(n):
            at = slice(q * kloc, (q + 1) * kloc)
            wave = jnp.dot(panel[place, :], weights[:, at], preferred_element_type=f32)
            res[wplace, at] = jnp.max(wave.reshape(wspan, TSTEP, kloc), axis=1)
        for d in range(1, n):
            result_copy(t, lax.rem(z + d, n), z, odd).start()
        home[z, wplace, :] = res[wplace, own]
        return carry

    lax.fori_loop(0, CHUNKS, compute, 0)

    def arrive(t, carry):
        for d in range(1, n):
            source = lax.rem(z + d, n)
            result_copy(t, source, source, lax.rem(source, 2)).wait_recv()
        return carry

    blocks = slip[z, width : width + META, :].astype(f32)[META // 2 : META // 2 + 1, :]
    pair = jnp.minimum(blocks, float(n - 2)).astype(jnp.int32)
    parity = lax.rem(pair, 2)
    holders = (pair + parity, pair + 1 - parity)

    def maxima(h, begin, end):
        total = home[h, begin:end, :]
        for source in range(h + 2, n, 2):
            total = jnp.where(holders[h] == source, home[source, begin:end, :], total)
        return total

    windows = 2 * whalf
    for copy in point_copies:
        copy.wait()
    code = jnp.broadcast_to(points[0, 0:1, :], (LANES, windows)).T
    codes = jnp.concatenate([code] * (kloc // LANES), axis=1)

    lax.fori_loop(0, CHUNKS // 2, arrive, 0)
    low = jnp.finfo(f32).min
    head = jnp.where(codes[0:MOST, :] == codes[0:1, :], maxima(0, 0, MOST), low)
    tail = jnp.where(
        codes[windows - MOST :, :] == codes[windows - 1 :, :], maxima(1, whalf - MOST, whalf), low
    )
    edge[0] = jnp.broadcast_to(jnp.max(head, axis=0, keepdims=True), (8, kloc))
    edge[3] = jnp.broadcast_to(jnp.max(tail, axis=0, keepdims=True), (8, kloc))
    edge_copies = row_copies(edge.at[0], edge.at[3], edge, esend, erecv)
    for copy in edge_copies:
        copy.start()

    lax.fori_loop(CHUNKS // 2, CHUNKS, arrive, 0)
    for copy in edge_copies:
        copy.wait()
    peak = jnp.concatenate([maxima(0, 0, whalf), maxima(1, 0, whalf)], axis=0)
    line = lax.broadcasted_iota(jnp.int32, code.shape, 0)
    masks = []
    step = 1
    while step < MOST:
        before = jnp.logical_and(pltpu.roll(code, step, 0) == code, line >= step)
        after = jnp.logical_and(
            pltpu.roll(code, windows - step, 0) == code, line < windows - step
        )
        masks.append((step, before, after))
        step *= 2
    from_left = jnp.logical_and(code == points[1, 0:1, windows - 1 : windows], me > 0)
    from_right = jnp.logical_and(code == points[2, 0:1, 0:1], me < count - 1)
    for q in range(kloc // LANES):
        at = slice(q * LANES, (q + 1) * LANES)
        forward = peak[:, at]
        backward = forward
        for step, before, after in masks:
            forward = jnp.where(before, jnp.maximum(forward, pltpu.roll(forward, step, 0)), forward)
            moved = pltpu.roll(backward, windows - step, 0)
            backward = jnp.where(after, jnp.maximum(backward, moved), backward)
        both = jnp.maximum(forward, backward)
        both = jnp.where(from_left, jnp.maximum(both, edge[1, 0:1, at]), both)
        both = jnp.where(from_right, jnp.maximum(both, edge[2, 0:1, at]), both)
        out_ref[at, :] = both.T

    for d in range(1, n):
        slip_copy(lax.rem(z + d, n), z).wait_send()
    for d in range(1, planes):
        plane_copy(lax.rem(chip + d, planes), chip).wait_send()

    def finish(t, carry):
        @pl.when(z > 0)
        def _():
            green_copy(0, t, 1 - odd).wait_send()

        @pl.when(z < n - 1)
        def _():
            green_copy(1, t, 1 - odd).wait_send()

        for d in range(1, n):
            result_copy(t, lax.rem(z + d, n), z, odd).wait_send()
        return carry

    lax.fori_loop(0, CHUNKS, finish, 0)


def paired(greens, slip_values, rupture_ids, win_point):
    n, count = lax.axis_size("cols"), lax.axis_size("rows")
    width, rows = greens.shape
    kloc, slots = slip_values.shape
    windows = win_point.shape[0]
    total = n * kloc
    half = windows // 2
    share = kloc // (count // 2)
    bf16, f32 = jnp.bfloat16, jnp.float32
    dma = pltpu.SemaphoreType.DMA
    return pl.pallas_call(
        functools.partial(kernel, n, count),
        out_shape=jax.ShapeDtypeStruct((kloc, windows), f32),
        in_specs=[pl.BlockSpec(memory_space=pl.ANY)] * 4,
        out_specs=pl.BlockSpec(memory_space=pltpu.VMEM),
        scratch_shapes=[
            pltpu.VMEM((width, rows), bf16),
            pltpu.VMEM((share, slots), bf16),
            pltpu.VMEM((share, slots), jnp.int32),
            pltpu.VMEM((1, windows), jnp.int32),
            pltpu.VMEM((rows // 2, 3 * width), bf16),
            pltpu.VMEM((rows // 2, width), bf16),
            pltpu.VMEM((n, width + META, kloc), bf16),
            pltpu.VMEM((3 * width, total), bf16),
            pltpu.VMEM((half, total), f32),
            pltpu.VMEM((n, half, kloc), f32),
            pltpu.VMEM((4, 8, kloc), f32),
            pltpu.VMEM((3, 8, windows), f32),
            dma((2, CHUNKS)), dma((3,)),
            dma((2, CHUNKS)), dma((2, CHUNKS)),
            dma((n,)), dma((n,)),
            dma((count // 2,)), dma((count // 2,)),
            dma((CHUNKS, n)), dma((CHUNKS, n)),
            dma((2,)), dma((2,)), dma((2,)), dma((2,)),
        ],
        compiler_params=pltpu.CompilerParams(
            collective_id=0, has_side_effects=True, vmem_limit_bytes=56 * 1024 * 1024
        ),
        cost_estimate=pl.CostEstimate(
            flops=3 * width * rows * total, bytes_accessed=4 * width * rows, transcendentals=0
        ),
    )(greens, slip_values, rupture_ids, win_point.reshape(1, windows))


def fits(mesh, greens, slip_values, win_point):
    n, count = mesh.shape["cols"], mesh.shape["rows"]
    width, kloc = greens.shape[0] // n, slip_values.shape[0] // n
    rows, windows = greens.shape[1] // count, win_point.shape[0] // count
    return (
        n >= 2
        and count >= 4
        and count % 2 == 0
        and width == LANES
        and slip_values.shape[1] == width
        and windows == LANES == 4 * MOST
        and rows == windows * TSTEP
        and kloc == LANES * (count // 2)
    )


def solution(mesh):
    in_specs = (P("cols", "rows"), P("cols", None), P("cols", None), P("rows"))
    out_specs = P("cols", "rows")

    def run(greens, slip_values, rupture_ids, win_point):
        local = paired if fits(mesh, greens, slip_values, win_point) else general
        return jax.shard_map(
            local, mesh=mesh, in_specs=in_specs, out_specs=out_specs, check_vma=False
        )(greens, slip_values, rupture_ids, win_point)

    return run
```

profile of v0, /device:TPU:1, one launch (start us, length us, event | category | flops | bytes accessed | tf_op | source)
XLA Modules:
  0.0 48.3 jit_solution(2410723336525697121)
XLA Ops:
  0.0 46.6 %shard_map.46 = f32[512,128]{1,0:T(8,128)} custom-call(bf16[128,8192]{1,0:T(8,128)(2,1)} %g_hbm.1, bf16[512,128]{1,0:T(8,128)(2,1)} %v_hbm.1, s32[512,128]{1,0:T(8,128)} %id_hbm.1, s32[1,128]{1,0:T(1,128)} %bitcast.1), custom_call_target="tpu_custom_call" | custom-call | flops 6442450944 | bytes 4194304 | tf_op jit(solution)/shard_map/pallas_call | solution.py:410
  46.6 1.7 %copy.6 = f32[512,128]{1,0:T(8,128)} copy(f32[512,128]{1,0:T(8,128)} %shard_map.46) | data formatting | bytes 524288
where the time goes:
time: 48.4 us; the launch traced here: 48.3 us
  Pallas kernels  46.6 us (96%)
  local copies, waits for them, and re-layouts  1.67 us (3%)
    pallas_call x1, Pallas kernels, paired(): pl.pallas_call(functools.partial(kernel, n, count), out_shape=jax.ShapeDt...  46.6 us
    unnamed x1, local copies, waits for them, and re-layouts  1.67 us

commit v1 on v0

--- a/solution.py
+++ b/solution.py
@@ -13,6 +13,9 @@
 LANES = 128
 META = 16
 CHUNKS = 8
+PAIRS = CHUNKS // 2
+REACH = 14.0
+CODES = 32767.0
 MESH = pl.DeviceIdType.MESH
 
 
@@ -113,7 +116,7 @@
 
 def kernel(
     n, count, g_hbm, v_hbm, id_hbm, wp_hbm, out_ref,
-    g_ref, v_ref, id_ref, wp_ref, panel, sent, slip, weights, res, home, edge, points,
+    g_ref, v_ref, id_ref, wp_ref, panel, sent, slip, weights, res, codes_out, home, edge, points,
     gload, load, gsend, grecv, zsend, zrecv, psend, precv, rsend, rrecv, wsend, wrecv, esend, erecv,
 ):
     f32, bf16 = jnp.float32, jnp.bfloat16
@@ -143,6 +146,9 @@
 
     def chunk(parity, t):
         return t + parity * (CHUNKS - 1 - 2 * t)
+
+    def couple(parity, t):
+        return t + parity * (PAIRS - 1 - 2 * t)
 
     def columns(parity, t):
         return pl.ds(pl.multiple_of(parity * half + chunk(parity, t) * span, span), span)
@@ -178,9 +184,21 @@
     slip[z, 0:width, mine] = values.T.astype(bf16)
     shift_rows = shift.astype(f32).T[0:META, :]
     block_rows = block.astype(f32).T[0:META, :]
-    first = lax.broadcasted_iota(jnp.int32, (META, share), 0) < META // 2
-    slip[z, width : width + META, mine] = jnp.where(first, shift_rows, block_rows).astype(bf16)
     points[0] = jnp.broadcast_to(wp_ref[...].astype(f32), (8, wp_ref.shape[1]))
+
+    def loudest(t, peak):
+        for which in range(2):
+            green_load(which, t).wait()
+            piece = jnp.abs(g_ref[:, columns(1 - odd if which == 0 else odd, t)].astype(f32))
+            for at in range(0, span, share):
+                peak = jnp.maximum(peak, piece[:, at : at + share])
+        return peak
+
+    top = lax.fori_loop(0, CHUNKS, loudest, jnp.zeros((width, share), f32))
+    top = jnp.max(jnp.max(top, axis=0, keepdims=True), axis=1, keepdims=True)
+    line = lax.broadcasted_iota(jnp.int32, (META, share), 0)
+    meta = jnp.where(line < META // 4, shift_rows, jnp.where(line < META // 2, top, block_rows))
+    slip[z, width : width + META, mine] = meta.astype(bf16)
 
     pl.semaphore_wait(barrier, n - 1 + planes - 1 + 2)
 
@@ -208,9 +226,9 @@
         )
 
     def result_copy(t, target, source, parity):
-        place = pl.ds(pl.multiple_of(chunk(parity, t) * wspan, wspan), wspan)
+        place = pl.ds(pl.multiple_of(couple(parity, t) * 2 * wspan, 2 * wspan), 2 * wspan)
         return pltpu.make_async_remote_copy(
-            src_ref=res.at[place, pl.ds(pl.multiple_of(target * kloc, kloc), kloc)],
+            src_ref=codes_out.at[place, pl.ds(pl.multiple_of(target * kloc, kloc), kloc)],
             dst_ref=home.at[source, place, :],
             send_sem=rsend.at[t, target], recv_sem=rrecv.at[t, source],
             device_id={"cols": target}, device_id_type=MESH,
@@ -231,7 +249,6 @@
         slip_copy(lax.rem(z + d, n), z).start()
 
     def send(t, carry):
-        green_load(0, t).wait()
         place = pl.ds(pl.multiple_of(chunk(1 - odd, t) * span, span), span)
         sent[place, :] = g_ref[:, columns(1 - odd, t)].T
 
@@ -256,7 +273,6 @@
         plane_copy(lax.rem(chip + d, planes), chip).start()
 
     def keep(t, carry):
-        green_load(1, t).wait()
         place = pl.ds(pl.multiple_of(chunk(odd, t) * span, span), span)
         panel[place, width : 2 * width] = g_ref[:, columns(odd, t)].T
         return carry
@@ -289,28 +305,47 @@
             weights[i * width : (i + 1) * width, at] = dense.astype(bf16)
 
     own = pl.ds(pl.multiple_of(z * kloc, kloc), kloc)
-
-    def compute(t, carry):
-        @pl.when(z > 0)
-        def _():
-            green_copy(1, t, odd).wait_recv()
-
-        @pl.when(z < n - 1)
-        def _():
-            green_copy(0, t, odd).wait_recv()
-
-        place = pl.ds(pl.multiple_of(chunk(odd, t) * span, span), span)
-        wplace = pl.ds(pl.multiple_of(chunk(odd, t) * wspan, wspan), wspan)
-        for q in range(n):
-            at = slice(q * kloc, (q + 1) * kloc)
-            wave = jnp.dot(panel[place, :], weights[:, at], preferred_element_type=f32)
-            res[wplace, at] = jnp.max(wave.reshape(wspan, TSTEP, kloc), axis=1)
+    bound = slip[0, width : width + META, mine].astype(f32)[META // 4 : META // 4 + 1, 0:1]
+    for q in range(1, n):
+        other = slip[q, width : width + META, mine].astype(f32)[META // 4 : META // 4 + 1, 0:1]
+        bound = jnp.maximum(bound, other)
+    bound = jnp.maximum(bound * (4.0 * width), 1e-30)
+
+    def encode(value):
+        level = jnp.log(jnp.abs(value) / bound) * (CODES / REACH) + CODES
+        level = (jnp.clip(level, 0.0, CODES) + 0.5).astype(jnp.int32)
+        return jnp.where(value < 0.0, -level, level).astype(jnp.int16)
+
+    def decode(code):
+        level = code.astype(jnp.int32).astype(f32)
+        size = jnp.exp((jnp.abs(level) - CODES) * (REACH / CODES)) * bound
+        return jnp.where(level > 0.0, size, jnp.where(level < 0.0, -size, 0.0))
+
+    def compute(pair_step, carry):
+        for part in range(2):
+            t = pair_step * 2 + part
+
+            @pl.when(z > 0)
+            def _():
+                green_copy(1, t, odd).wait_recv()
+
+            @pl.when(z < n - 1)
+            def _():
+                green_copy(0, t, odd).wait_recv()
+
+            place = pl.ds(pl.multiple_of(chunk(odd, t) * span, span), span)
+            wplace = pl.ds(pl.multiple_of(chunk(odd, t) * wspan, wspan), wspan)
+            for q in range(n):
+                at = slice(q * kloc, (q + 1) * kloc)
+                wave = jnp.dot(panel[place, :], weights[:, at], preferred_element_type=f32)
+                res[wplace, at] = jnp.max(wave.reshape(wspan, TSTEP, kloc), axis=1)
+        both = pl.ds(pl.multiple_of(couple(odd, pair_step) * 2 * wspan, 2 * wspan), 2 * wspan)
+        codes_out[both, :] = encode(res[both, :])
         for d in range(1, n):
-            result_copy(t, lax.rem(z + d, n), z, odd).start()
-        home[z, wplace, :] = res[wplace, own]
+            result_copy(pair_step, lax.rem(z + d, n), z, odd).start()
         return carry
 
-    lax.fori_loop(0, CHUNKS, compute, 0)
+    lax.fori_loop(0, PAIRS, compute, 0)
 
     def arrive(t, carry):
         for d in range(1, n):
@@ -324,10 +359,11 @@
     holders = (pair + parity, pair + 1 - parity)
 
     def maxima(h, begin, end):
-        total = home[h, begin:end, :]
+        total = home[h, begin:end, :].astype(jnp.int32)
         for source in range(h + 2, n, 2):
-            total = jnp.where(holders[h] == source, home[source, begin:end, :], total)
-        return total
+            other = home[source, begin:end, :].astype(jnp.int32)
+            total = jnp.where(holders[h] == source, other, total)
+        return jnp.where(holders[h] == z, res[begin:end, own], decode(total))
 
     windows = 2 * whalf
     for copy in point_copies:
@@ -335,7 +371,7 @@
     code = jnp.broadcast_to(points[0, 0:1, :], (LANES, windows)).T
     codes = jnp.concatenate([code] * (kloc // LANES), axis=1)
 
-    lax.fori_loop(0, CHUNKS // 2, arrive, 0)
+    lax.fori_loop(0, PAIRS // 2, arrive, 0)
     low = jnp.finfo(f32).min
     head = jnp.where(codes[0:MOST, :] == codes[0:1, :], maxima(0, 0, MOST), low)
     tail = jnp.where(
@@ -347,7 +383,7 @@
     for copy in edge_copies:
         copy.start()
 
-    lax.fori_loop(CHUNKS // 2, CHUNKS, arrive, 0)
+    lax.fori_loop(PAIRS // 2, PAIRS, arrive, 0)
     for copy in edge_copies:
         copy.wait()
     peak = jnp.concatenate([maxima(0, 0, whalf), maxima(1, 0, whalf)], axis=0)
@@ -390,11 +426,16 @@
         def _():
             green_copy(1, t, 1 - odd).wait_send()
 
+        return carry
+
+    lax.fori_loop(0, CHUNKS, finish, 0)
+
+    def settle(t, carry):
         for d in range(1, n):
             result_copy(t, lax.rem(z + d, n), z, odd).wait_send()
         return carry
 
-    lax.fori_loop(0, CHUNKS, finish, 0)
+    lax.fori_loop(0, PAIRS, settle, 0)
 
 
 def paired(greens, slip_values, rupture_ids, win_point):
@@ -410,7 +451,7 @@
     return pl.pallas_call(
         functools.partial(kernel, n, count),
         out_shape=jax.ShapeDtypeStruct((kloc, windows), f32),
-        in_specs=[pl.BlockSpec(memory_space=pl.ANY)] * 4,
+        in_specs=[pl.BlockSpec(memory_space=pltpu.HBM)] * 4,
         out_specs=pl.BlockSpec(memory_space=pltpu.VMEM),
         scratch_shapes=[
             pltpu.VMEM((width, rows), bf16),
@@ -422,14 +463,15 @@
             pltpu.VMEM((n, width + META, kloc), bf16),
             pltpu.VMEM((3 * width, total), bf16),
             pltpu.VMEM((half, total), f32),
-            pltpu.VMEM((n, half, kloc), f32),
+            pltpu.VMEM((half, total), jnp.int16),
+            pltpu.VMEM((n, half, kloc), jnp.int16),
             pltpu.VMEM((4, 8, kloc), f32),
             pltpu.VMEM((3, 8, windows), f32),
             dma((2, CHUNKS)), dma((3,)),
             dma((2, CHUNKS)), dma((2, CHUNKS)),
             dma((n,)), dma((n,)),
             dma((count // 2,)), dma((count // 2,)),
-            dma((CHUNKS, n)), dma((CHUNKS, n)),
+            dma((PAIRS, n)), dma((PAIRS, n)),
             dma((2,)), dma((2,)), dma((2,)), dma((2,)),
         ],
         compiler_params=pltpu.CompilerParams(

time: 48.4 us -> 44.7 us (0.924)
  Pallas kernels: 46.6 us -> 42.9 us
    pallas_call x1, Pallas kernels: 46.6 us -> 42.9 us  [paired(): pl.pallas_call(functools.partial(kernel, n, count), out_shape=jax.ShapeDt...]
where the time goes in v1:
time: 44.7 us; the launch traced here: 44.6 us
  Pallas kernels  42.9 us (96%)
  local copies, waits for them, and re-layouts  1.67 us (4%)
    pallas_call x1, Pallas kernels, paired(): pl.pallas_call(functools.partial(kernel, n, count), out_shape=jax.ShapeDt...  42.9 us
    unnamed x1, local copies, waits for them, and re-layouts  1.67 us

profile of v1, /device:TPU:1, one launch (start us, length us, event | category | flops | bytes accessed | tf_op | source)
XLA Modules:
  0.0 44.6 jit_solution(14218024094641807775)
XLA Ops:
  0.0 42.9 %shard_map.46 = f32[512,128]{1,0:T(8,128)} custom-call(bf16[128,8192]{1,0:T(8,128)(2,1)} %g_hbm.1, bf16[512,128]{1,0:T(8,128)(2,1)} %v_hbm.1, s32[512,128]{1,0:T(8,128)} %id_hbm.1, s32[1,128]{1,0:T(1,128)} %bitcast.1), custom_call_target="tpu_custom_call" | custom-call | flops 6442450944 | bytes 4194304 | tf_op jit(solution)/shard_map/pallas_call | solution.py:451
  42.9 1.7 %copy.6 = f32[512,128]{1,0:T(8,128)} copy(f32[512,128]{1,0:T(8,128)} %shard_map.46) | data formatting | bytes 524288

commit v2 on v1

--- a/solution.py
+++ b/solution.py
@@ -116,8 +116,8 @@
 
 def kernel(
     n, count, g_hbm, v_hbm, id_hbm, wp_hbm, out_ref,
-    g_ref, v_ref, id_ref, wp_ref, panel, sent, slip, weights, res, codes_out, home, edge, points,
-    gload, load, gsend, grecv, zsend, zrecv, psend, precv, rsend, rrecv, wsend, wrecv, esend, erecv,
+    g_ref, v_ref, id_ref, wp_ref, panel, sent, slip, weights, res, codes_out, home, edge, points, bounds,
+    gload, load, gsend, grecv, zsend, zrecv, hsend, hrecv, bsend, brecv, psend, precv, rsend, rrecv, wsend, wrecv, esend, erecv,
 ):
     f32, bf16 = jnp.float32, jnp.bfloat16
     me = lax.axis_index("rows")
@@ -164,11 +164,89 @@
         pltpu.make_async_copy(v_hbm.at[mine, :], v_ref, load.at[1]),
         pltpu.make_async_copy(wp_hbm, wp_ref, load.at[2]),
     ]
+    green_load(0, 0).start()
     for copy in loads:
         copy.start()
-    for which in range(2):
-        for t in range(CHUNKS):
-            green_load(which, t).start()
+    for t in range(CHUNKS):
+        for which in range(2):
+            if t > 0 or which > 0:
+                green_load(which, t).start()
+
+    def slip_copy(target, source):
+        return pltpu.make_async_remote_copy(
+            src_ref=slip.at[source, chip], dst_ref=slip.at[source, chip],
+            send_sem=zsend.at[target], recv_sem=zrecv.at[source],
+            device_id={"cols": target}, device_id_type=MESH,
+        )
+
+    def sibling_copy(source):
+        return pltpu.make_async_remote_copy(
+            src_ref=slip.at[source, chip], dst_ref=slip.at[source, chip],
+            send_sem=hsend.at[source], recv_sem=hrecv.at[source],
+            device_id={"rows": chip * 2 + 1 - core}, device_id_type=MESH,
+        )
+
+    def bound_copy(target, source):
+        return pltpu.make_async_remote_copy(
+            src_ref=bounds.at[source], dst_ref=bounds.at[source],
+            send_sem=bsend.at[target], recv_sem=brecv.at[source],
+            device_id={"cols": target}, device_id_type=MESH,
+        )
+
+    def plane_copy(target, source):
+        place = slip.at[:, source]
+        return pltpu.make_async_remote_copy(
+            src_ref=place, dst_ref=place, send_sem=psend.at[target], recv_sem=precv.at[source],
+            device_id={"rows": target * 2 + core}, device_id_type=MESH,
+        )
+
+    def green_copy(side, t, parity):
+        place = pl.ds(pl.multiple_of(chunk(parity, t) * span, span), span)
+        to, slot = (lax.rem(z + n - 1, n), 2) if side == 0 else (lax.rem(z + 1, n), 0)
+        return pltpu.make_async_remote_copy(
+            src_ref=sent.at[place, :], dst_ref=panel.at[slot, place, :],
+            send_sem=gsend.at[side, t], recv_sem=grecv.at[side, t],
+            device_id={"cols": to}, device_id_type=MESH,
+        )
+
+    def result_copy(t, target, source, parity):
+        place = pl.ds(pl.multiple_of(couple(parity, t) * 2 * wspan, 2 * wspan), 2 * wspan)
+        return pltpu.make_async_remote_copy(
+            src_ref=codes_out.at[place, pl.ds(pl.multiple_of(target * kloc, kloc), kloc)],
+            dst_ref=home.at[source, place, :],
+            send_sem=rsend.at[t, target], recv_sem=rrecv.at[t, source],
+            device_id={"cols": target}, device_id_type=MESH,
+        )
+
+    def row_copies(src_left, src_right, buffer, send, recv):
+        to_left = pltpu.make_async_remote_copy(
+            src_ref=src_left, dst_ref=buffer.at[2], send_sem=send.at[0], recv_sem=recv.at[0],
+            device_id={"rows": left}, device_id_type=MESH,
+        )
+        to_right = pltpu.make_async_remote_copy(
+            src_ref=src_right, dst_ref=buffer.at[1], send_sem=send.at[1], recv_sem=recv.at[1],
+            device_id={"rows": right}, device_id_type=MESH,
+        )
+        return to_left, to_right
+
+    def send(t, carry):
+        place = pl.ds(pl.multiple_of(chunk(1 - odd, t) * span, span), span)
+        sent[place, :] = g_ref[:, columns(1 - odd, t)].T
+
+        @pl.when(z > 0)
+        def _():
+            green_copy(0, t, 1 - odd).start()
+
+        @pl.when(z < n - 1)
+        def _():
+            green_copy(1, t, 1 - odd).start()
+
+        return carry
+
+    green_load(0, 0).wait()
+    pl.semaphore_wait(barrier, n - 1 + planes - 1 + 2)
+    send(0, 0)
+
     for copy in loads:
         copy.wait()
     ids = id_ref[...]
@@ -181,120 +259,80 @@
         moved = pltpu.roll(values, step, 1)
         values = jnp.where(lax.rem(shift // step, 2) == 1, moved, values)
         step *= 2
-    slip[z, 0:width, mine] = values.T.astype(bf16)
+    slip[z, chip, 0:width, :] = values.T.astype(bf16)
     shift_rows = shift.astype(f32).T[0:META, :]
     block_rows = block.astype(f32).T[0:META, :]
-    points[0] = jnp.broadcast_to(wp_ref[...].astype(f32), (8, wp_ref.shape[1]))
+    first = lax.broadcasted_iota(jnp.int32, (META, share), 0) < META // 2
+    slip[z, chip, width : width + META, :] = jnp.where(first, shift_rows, block_rows).astype(bf16)
+    for d in range(1, n):
+
+        @pl.when(core == d % 2)
+        def _():
+            slip_copy(lax.rem(z + d, n), z).start()
 
     def loudest(t, peak):
-        for which in range(2):
-            green_load(which, t).wait()
-            piece = jnp.abs(g_ref[:, columns(1 - odd if which == 0 else odd, t)].astype(f32))
+        @pl.when(t > 0)
+        def _():
+            green_load(0, t).wait()
+
+        green_load(1, t).wait()
+        for parity in range(2):
+            piece = jnp.abs(g_ref[:, columns(parity, t)].astype(f32))
             for at in range(0, span, share):
                 peak = jnp.maximum(peak, piece[:, at : at + share])
         return peak
 
     top = lax.fori_loop(0, CHUNKS, loudest, jnp.zeros((width, share), f32))
     top = jnp.max(jnp.max(top, axis=0, keepdims=True), axis=1, keepdims=True)
-    line = lax.broadcasted_iota(jnp.int32, (META, share), 0)
-    meta = jnp.where(line < META // 4, shift_rows, jnp.where(line < META // 2, top, block_rows))
-    slip[z, width : width + META, mine] = meta.astype(bf16)
-
-    pl.semaphore_wait(barrier, n - 1 + planes - 1 + 2)
-
-    def slip_copy(target, source):
-        return pltpu.make_async_remote_copy(
-            src_ref=slip.at[z, :, mine], dst_ref=slip.at[z, :, mine],
-            send_sem=zsend.at[target], recv_sem=zrecv.at[source],
-            device_id={"cols": target}, device_id_type=MESH,
-        )
-
-    def plane_copy(target, source):
-        place = slip.at[:, :, pl.ds(pl.multiple_of(source * share, share), share)]
-        return pltpu.make_async_remote_copy(
-            src_ref=place, dst_ref=place, send_sem=psend.at[target], recv_sem=precv.at[source],
-            device_id={"rows": target * 2 + core}, device_id_type=MESH,
-        )
-
-    def green_copy(side, t, parity):
-        place = pl.ds(pl.multiple_of(chunk(parity, t) * span, span), span)
-        to, at = (lax.rem(z + n - 1, n), 2 * width) if side == 0 else (lax.rem(z + 1, n), 0)
-        return pltpu.make_async_remote_copy(
-            src_ref=sent.at[place, :], dst_ref=panel.at[place, pl.ds(at, width)],
-            send_sem=gsend.at[side, t], recv_sem=grecv.at[side, t],
-            device_id={"cols": to}, device_id_type=MESH,
-        )
-
-    def result_copy(t, target, source, parity):
-        place = pl.ds(pl.multiple_of(couple(parity, t) * 2 * wspan, 2 * wspan), 2 * wspan)
-        return pltpu.make_async_remote_copy(
-            src_ref=codes_out.at[place, pl.ds(pl.multiple_of(target * kloc, kloc), kloc)],
-            dst_ref=home.at[source, place, :],
-            send_sem=rsend.at[t, target], recv_sem=rrecv.at[t, source],
-            device_id={"cols": target}, device_id_type=MESH,
-        )
-
-    def row_copies(src_left, src_right, buffer, send, recv):
-        to_left = pltpu.make_async_remote_copy(
-            src_ref=src_left, dst_ref=buffer.at[2], send_sem=send.at[0], recv_sem=recv.at[0],
-            device_id={"rows": left}, device_id_type=MESH,
-        )
-        to_right = pltpu.make_async_remote_copy(
-            src_ref=src_right, dst_ref=buffer.at[1], send_sem=send.at[1], recv_sem=recv.at[1],
-            device_id={"rows": right}, device_id_type=MESH,
-        )
-        return to_left, to_right
-
+    bounds[z] = jnp.broadcast_to(top, (8, share))
     for d in range(1, n):
-        slip_copy(lax.rem(z + d, n), z).start()
-
-    def send(t, carry):
-        place = pl.ds(pl.multiple_of(chunk(1 - odd, t) * span, span), span)
-        sent[place, :] = g_ref[:, columns(1 - odd, t)].T
-
-        @pl.when(z > 0)
-        def _():
-            green_copy(0, t, 1 - odd).start()
-
-        @pl.when(z < n - 1)
-        def _():
-            green_copy(1, t, 1 - odd).start()
-
-        return carry
-
-    lax.fori_loop(0, CHUNKS, send, 0)
-
+        bound_copy(lax.rem(z + d, n), z).start()
+
+    lax.fori_loop(1, CHUNKS, send, 0)
+
+    points[0] = jnp.broadcast_to(wp_ref[...].astype(f32), (8, wp_ref.shape[1]))
     point_copies = row_copies(points.at[0], points.at[0], points, wsend, wrecv)
     for copy in point_copies:
         copy.start()
     for d in range(1, n):
-        slip_copy(lax.rem(z + d, n), lax.rem(z + d, n)).wait_recv()
+        source = lax.rem(z + d, n)
+
+        @pl.when(core == (n - d) % 2)
+        def _():
+            slip_copy(source, source).wait_recv()
+            sibling_copy(source).start()
+
+        @pl.when(core != (n - d) % 2)
+        def _():
+            sibling_copy(source).wait_recv()
+
     for d in range(1, planes):
         plane_copy(lax.rem(chip + d, planes), chip).start()
 
     def keep(t, carry):
         place = pl.ds(pl.multiple_of(chunk(odd, t) * span, span), span)
-        panel[place, width : 2 * width] = g_ref[:, columns(odd, t)].T
+        panel[1, place, :] = g_ref[:, columns(odd, t)].T
         return carry
 
     lax.fori_loop(0, CHUNKS, keep, 0)
 
     @pl.when(z == 0)
     def _():
-        panel[:, 0:width] = jnp.zeros((half, width), bf16)
+        panel[0] = jnp.zeros((half, width), bf16)
 
     @pl.when(z == n - 1)
     def _():
-        panel[:, 2 * width : 3 * width] = jnp.zeros((half, width), bf16)
+        panel[2] = jnp.zeros((half, width), bf16)
 
     for d in range(1, planes):
         source = lax.rem(chip + d, planes)
         plane_copy(source, source).wait_recv()
 
-    for q in range(n):
-        at = slice(q * kloc, (q + 1) * kloc)
-        folded = slip[q, 0:width, :].astype(f32)
-        meta = slip[q, width : width + META, :].astype(f32)
+    for place in range(n * planes):
+        at = slice(place * share, (place + 1) * share)
+        q, c = place // planes, place % planes
+        folded = slip[q, c, 0:width, :].astype(f32)
+        meta = slip[q, c, width : width + META, :].astype(f32)
         shifts, blocks = meta[0:1, :], meta[META // 2 : META // 2 + 1, :]
         later = lax.broadcasted_iota(jnp.int32, folded.shape, 0).astype(f32) >= shifts
         upper = jnp.where(later, folded, 0.0)
@@ -305,10 +343,11 @@
             weights[i * width : (i + 1) * width, at] = dense.astype(bf16)
 
     own = pl.ds(pl.multiple_of(z * kloc, kloc), kloc)
-    bound = slip[0, width : width + META, mine].astype(f32)[META // 4 : META // 4 + 1, 0:1]
+    for d in range(1, n):
+        bound_copy(lax.rem(z + d, n), lax.rem(z + d, n)).wait_recv()
+    bound = bounds[0, 0:1, 0:1]
     for q in range(1, n):
-        other = slip[q, width : width + META, mine].astype(f32)[META // 4 : META // 4 + 1, 0:1]
-        bound = jnp.maximum(bound, other)
+        bound = jnp.maximum(bound, bounds[q, 0:1, 0:1])
     bound = jnp.maximum(bound * (4.0 * width), 1e-30)
 
     def encode(value):
@@ -335,9 +374,10 @@
 
             place = pl.ds(pl.multiple_of(chunk(odd, t) * span, span), span)
             wplace = pl.ds(pl.multiple_of(chunk(odd, t) * wspan, wspan), wspan)
+            piece = jnp.concatenate([panel[i, place, :] for i in range(3)], axis=1)
             for q in range(n):
                 at = slice(q * kloc, (q + 1) * kloc)
-                wave = jnp.dot(panel[place, :], weights[:, at], preferred_element_type=f32)
+                wave = jnp.dot(piece, weights[:, at], preferred_element_type=f32)
                 res[wplace, at] = jnp.max(wave.reshape(wspan, TSTEP, kloc), axis=1)
         both = pl.ds(pl.multiple_of(couple(odd, pair_step) * 2 * wspan, 2 * wspan), 2 * wspan)
         codes_out[both, :] = encode(res[both, :])
@@ -353,7 +393,13 @@
             result_copy(t, source, source, lax.rem(source, 2)).wait_recv()
         return carry
 
-    blocks = slip[z, width : width + META, :].astype(f32)[META // 2 : META // 2 + 1, :]
+    blocks = jnp.concatenate(
+        [
+            slip[z, c, width : width + META, :].astype(f32)[META // 2 : META // 2 + 1, :]
+            for c in range(planes)
+        ],
+        axis=1,
+    )
     pair = jnp.minimum(blocks, float(n - 2)).astype(jnp.int32)
     parity = lax.rem(pair, 2)
     holders = (pair + parity, pair + 1 - parity)
@@ -413,7 +459,17 @@
         out_ref[at, :] = both.T
 
     for d in range(1, n):
-        slip_copy(lax.rem(z + d, n), z).wait_send()
+        source = lax.rem(z + d, n)
+
+        @pl.when(core == d % 2)
+        def _():
+            slip_copy(source, z).wait_send()
+
+        @pl.when(core == (n - d) % 2)
+        def _():
+            sibling_copy(source).wait_send()
+
+        bound_copy(source, z).wait_send()
     for d in range(1, planes):
         plane_copy(lax.rem(chip + d, planes), chip).wait_send()
 
@@ -458,17 +514,20 @@
             pltpu.VMEM((share, slots), bf16),
             pltpu.VMEM((share, slots), jnp.int32),
             pltpu.VMEM((1, windows), jnp.int32),
-            pltpu.VMEM((rows // 2, 3 * width), bf16),
+            pltpu.VMEM((3, rows // 2, width), bf16),
             pltpu.VMEM((rows // 2, width), bf16),
-            pltpu.VMEM((n, width + META, kloc), bf16),
+            pltpu.VMEM((n, count // 2, width + META, share), bf16),
             pltpu.VMEM((3 * width, total), bf16),
             pltpu.VMEM((half, total), f32),
             pltpu.VMEM((half, total), jnp.int16),
             pltpu.VMEM((n, half, kloc), jnp.int16),
             pltpu.VMEM((4, 8, kloc), f32),
             pltpu.VMEM((3, 8, windows), f32),
+            pltpu.VMEM((n, 8, share), f32),
             dma((2, CHUNKS)), dma((3,)),
             dma((2, CHUNKS)), dma((2, CHUNKS)),
+            dma((n,)), dma((n,)),
+            dma((n,)), dma((n,)),
             dma((n,)), dma((n,)),
             dma((count // 2,)), dma((count // 2,)),
             dma((PAIRS, n)), dma((PAIRS, n)),

time: 44.7 us -> 42.2 us (0.944)
  Pallas kernels: 42.9 us -> 40.4 us
    pallas_call x1, Pallas kernels: 42.9 us -> 40.4 us  [paired(): pl.pallas_call(functools.partial(kernel, n, count), out_shape=jax.ShapeDt...]
where the time goes in v2:
time: 42.2 us; the launch traced here: 42.1 us
  Pallas kernels  40.4 us (96%)
  local copies, waits for them, and re-layouts  1.67 us (4%)
    pallas_call x1, Pallas kernels, paired(): pl.pallas_call(functools.partial(kernel, n, count), out_shape=jax.ShapeDt...  40.4 us
    unnamed x1, local copies, waits for them, and re-layouts  1.67 us

profile of v2, /device:TPU:1, one launch (start us, length us, event | category | flops | bytes accessed | tf_op | source)
XLA Modules:
  0.0 42.1 jit_solution(11024695137174060670)
XLA Ops:
  0.0 40.4 %shard_map.46 = f32[512,128]{1,0:T(8,128)} custom-call(bf16[128,8192]{1,0:T(8,128)(2,1)} %g_hbm.1, bf16[512,128]{1,0:T(8,128)(2,1)} %v_hbm.1, s32[512,128]{1,0:T(8,128)} %id_hbm.1, s32[1,128]{1,0:T(1,128)} %bitcast.1), custom_call_target="tpu_custom_call" | custom-call | flops 6442450944 | bytes 4194304 | tf_op jit(solution)/shard_map/pallas_call | solution.py:507
  40.4 1.7 %copy.6 = f32[512,128]{1,0:T(8,128)} copy(f32[512,128]{1,0:T(8,128)} %shard_map.46) | data formatting | bytes 524288

commit v3 on v2

--- a/solution.py
+++ b/solution.py
@@ -12,7 +12,7 @@
 MOST = 32
 LANES = 128
 META = 16
-CHUNKS = 8
+CHUNKS = 4
 PAIRS = CHUNKS // 2
 REACH = 14.0
 CODES = 32767.0

time: 42.2 us -> 43.1 us (1.021)
  the two profiles are of different devices: /device:TPU:1 before, /device:TPU:0 now
where the time goes in v3:
time: 43.1 us; the launch traced here: 43 us
  Pallas kernels  41.3 us (96%)
  local copies, waits for them, and re-layouts  1.67 us (4%)
    pallas_call x1, Pallas kernels, paired(): pl.pallas_call(functools.partial(kernel, n, count), out_shape=jax.ShapeDt...  41.3 us
    unnamed x1, local copies, waits for them, and re-layouts  1.67 us

profile of v3, /device:TPU:0, one launch (start us, length us, event | category | flops | bytes accessed | tf_op | source)
XLA Modules:
  0.0 43.0 jit_solution(2337482077719326024)
XLA Ops:
  0.0 41.3 %shard_map.46 = f32[512,128]{1,0:T(8,128)} custom-call(bf16[128,8192]{1,0:T(8,128)(2,1)} %g_hbm.1, bf16[512,128]{1,0:T(8,128)(2,1)} %v_hbm.1, s32[512,128]{1,0:T(8,128)} %id_hbm.1, s32[1,128]{1,0:T(1,128)} %bitcast.1), custom_call_target="tpu_custom_call" | custom-call | flops 6442450944 | bytes 4194304 | tf_op jit(solution)/shard_map/pallas_call | solution.py:507
  41.3 1.7 %copy.6 = f32[512,128]{1,0:T(8,128)} copy(f32[512,128]{1,0:T(8,128)} %shard_map.46) | data formatting | bytes 524288
